TPU v7x, 128 devices: a whole 4x4x4 slice. The times are simulated.
128 devices in a mesh: grp: 4 (over z), eig: 32 (over y, x, core).
Axes of the slice: x: 4, y: 4, z: 4, core: 2. Of those that a mesh axis runs over, the one named last changes fastest.
Arguments:
- out_grads: bfloat16 [1024, 14336], P(('grp', 'eig')), may hold values from -6 to 6
- activations: bfloat16 [1024, 8192], P(('grp', 'eig')), may hold values from -6 to 6
- grad_basis: bfloat16 [14336, 14336], P(None, 'eig'), may hold values from -0.046875 to 0.046875
- act_basis: bfloat16 [8192, 8192], P(None, 'eig'), may hold values from -0.0625 to 0.0625
- corrections: bfloat16 [14336, 8192], P('eig'), may hold values from 0.049804688 to 5
- query_left: bfloat16 [4, 32, 14336], P(None, None, 'eig'), may hold values from -0.0078125 to 0.0078125
- query_right: bfloat16 [4, 32, 8192], P(None, None, 'eig'), may hold values from -0.0625 to 0.0625
Outputs:
- scores: float32 [1024, 4], replicated
All inputs are finite; a program needn't handle non-finite values.
Results may differ from a plain program's by a relative error of at most 0.008.
Values may be sent and summed in bfloat16 or wider, within the bound.
A program may use at most 128 MiB of HBM per device.

v0:
```python
import jax
import jax.numpy as jnp
from jax import lax
from jax.sharding import PartitionSpec as P


def per_device(out_grads, activations, grad_basis, act_basis, corrections, query_left, query_right):
    grad_rot = jnp.dot(
        lax.all_gather(out_grads, "eig", axis=0, tiled=True),
        grad_basis,
        preferred_element_type=jnp.float32,
    )
    act_local = jnp.dot(
        lax.all_gather(activations, "eig", axis=0, tiled=True),
        act_basis,
        preferred_element_type=jnp.float32,
    ).astype(jnp.bfloat16)
    act_rot = lax.all_gather(act_local, "eig", axis=1, tiled=True)
    right_full = lax.all_gather(query_right, "eig", axis=2, tiled=True)

    def one_query(factors):
        left, right = factors
        product = lax.dot_general(
            left, right, (((0,), (0,)), ((), ())), preferred_element_type=jnp.float32
        )
        precond = (product / (corrections.astype(jnp.float32) + 0.1)).astype(jnp.bfloat16)
        applied = lax.dot_general(
            act_rot, precond, (((1,), (1,)), ((), ())), preferred_element_type=jnp.float32
        )
        return jnp.sum(applied * grad_rot, axis=1)

    partial_scores = lax.map(one_query, (query_left, right_full)).T
    summed = lax.psum(partial_scores, "eig")
    return lax.all_gather(summed, "grp", axis=0, tiled=True)


def solution(mesh):
    placed = (
        P(("grp", "eig"), None),
        P(("grp", "eig"), None),
        P(None, "eig"),
        P(None, "eig"),
        P("eig", None),
        P(None, None, "eig"),
        P(None, None, "eig"),
    )
    return jax.shard_map(per_device, mesh=mesh, in_specs=placed, out_specs=P(), check_vma=False)
```

profile of v0, /device:TPU:1, one launch (start us, length us, event | category | flops | bytes accessed | tf_op | source)
XLA Modules:
  0.0 322.1 jit_solution(196726388421690093)
XLA Ops:
  6.5 0.0 all-gather.7.cloned.1.call-start
  6.5 0.7 all-gather.7.cloned.1.call-update
  7.3 0.0 all-gather.11.cloned.1.call-start
  7.3 0.7 all-gather.11.cloned.1.call-update
  8.0 0.0 all-gather.5.cloned.1.call-start
  8.1 0.7 all-gather.5.cloned.1.call-update
  8.7 0.0 all-gather.9.cloned.1.call-start
  8.8 50.4 %all-gather.7.cloned.1.call-done = bf16[256,8192]{1,0:T(8,128)(2,1)} async-done(((bf16[8,8192]{1,0:T(8,128)(2,1)}), bf16[256,8192]{1,0:T(8,128)(2,1)}) %all-gather.7.cloned.1.call-update) | async-done | bytes 4194320 | tf_op jit(solution)/shard_map/all_gather | solution.py:14
  59.2 5.4 %convolution_convert_fusion = bf16[256,256]{1,0:T(8,128)(2,1)} fusion(bf16[256,8192]{1,0:T(8,128)(2,1)} %all-gather.7.cloned.1.call-done, bf16[8192,256]{1,0:T(8,128)(2,1)} %param.12), kind=kOutput, calls=%fused_computation.11 | convolution fusion | flops 1073807360 | bytes 8519680 | tf_op jit(solution)/shard_map/dot_general | solution.py:13
  64.6 0.0 all-gather.9.cloned.1.call-update
  64.6 47.0 %all-gather.11.cloned.1.call-done = bf16[256,14336]{1,0:T(8,128)(2,1)} async-done(((bf16[8,14336]{1,0:T(8,128)(2,1)}), bf16[256,14336]{1,0:T(8,128)(2,1)}) %all-gather.11.cloned.1.call-update) | async-done | bytes 7340048 | tf_op jit(solution)/shard_map/all_gather | solution.py:9
  111.7 9.6 %fusion.15 = f32[256,448]{0,1:T(8,128)S(1)} fusion(bf16[256,14336]{1,0:T(8,128)(2,1)} %all-gather.11.cloned.1.call-done, bf16[14336,448]{0,1:T(8,128)(2,1)} %param.11), kind=kOutput, calls=%fused_computation.12 | convolution fusion | flops 3288334336 | bytes 20643840 | tf_op jit(solution)/shard_map/dot_general | solution.py:8
  121.2 36.5 %all-gather.5.cloned.1.call-done = bf16[4,32,8192]{2,1,0:T(8,128)(2,1)} async-done(((bf16[4,32,256]{2,1,0:T(8,128)(2,1)}), bf16[4,32,8192]{2,1,0:T(8,128)(2,1)}) %all-gather.5.cloned.1.call-update) | async-done | bytes 2097168 | tf_op jit(solution)/shard_map/all_gather | solution.py:19
  157.8 50.6 %all-gather.9.cloned.1.call-done = bf16[256,8192]{1,0:T(8,128)(2,1)} async-done(((bf16[256,256]{1,0:T(8,128)(2,1)}), bf16[256,8192]{1,0:T(8,128)(2,1)}) %all-gather.9.cloned.1.call-update) | async-done | bytes 4194320 | tf_op jit(solution)/shard_map/all_gather | solution.py:18
  208.4 34.7 %while.10 = (s32[]{:T(128)}, f32[4,256]{1,0:T(4,128)S(1)}, bf16[4,32,448]{2,1,0:T(8,128)(2,1)}, bf16[4,32,8192]{2,1,0:T(8,128)(2,1)}, bf16[448,8192]{1,0:T(8,128...) while((s32[]{:T(128)}, f32[4,256]{1,0:T(4,128)S(1)}, ...), condition=%wide.region_2.3_spmd, body=%wide.region_0.2_spmd.sunk | while | flops 2128838400 | bytes 12554337 | solution.py:32
  208.4 8.6 %fusion.28 = f32[256]{0:T(256)S(1)} fusion(f32[256,448]{0,1:T(8,128)S(1)} %get-tuple-element.124, bf16[256,8192]{1,0:T(8,128)(2,1)} %get-tuple-element.123, bf16[448,8192]{1,0:T(8,128)(2,1)} %get-tuple-element.122, bf16[4,32,8192]{2,1,0:T(8,128)(2,1)} %get-tuple-element.121, s32[]{:T(128)} %get-tuple-element.109, ...), kind=kOutput, calls=%fused_computation.4.clone.1 | convolution fusion | flops 2128838400 | bytes 12552192 | tf_op jit(solution)/shard_map/while/body/eval_jaxpr/dot_general | solution.py:27
  217.1 8.6 %fusion.28 = f32[256]{0:T(256)S(1)} fusion(f32[256,448]{0,1:T(8,128)S(1)} %get-tuple-element.124, bf16[256,8192]{1,0:T(8,128)(2,1)} %get-tuple-element.123, bf16[448,8192]{1,0:T(8,128)(2,1)} %get-tuple-element.122, bf16[4,32,8192]{2,1,0:T(8,128)(2,1)} %get-tuple-element.121, s32[]{:T(128)} %get-tuple-element.109, ...), kind=kOutput, calls=%fused_computation.4.clone.1 | convolution fusion | flops 2128838400 | bytes 12552192 | tf_op jit(solution)/shard_map/while/body/eval_jaxpr/dot_general | solution.py:27
  225.8 8.6 %fusion.28 = f32[256]{0:T(256)S(1)} fusion(f32[256,448]{0,1:T(8,128)S(1)} %get-tuple-element.124, bf16[256,8192]{1,0:T(8,128)(2,1)} %get-tuple-element.123, bf16[448,8192]{1,0:T(8,128)(2,1)} %get-tuple-element.122, bf16[4,32,8192]{2,1,0:T(8,128)(2,1)} %get-tuple-element.121, s32[]{:T(128)} %get-tuple-element.109, ...), kind=kOutput, calls=%fused_computation.4.clone.1 | convolution fusion | flops 2128838400 | bytes 12552192 | tf_op jit(solution)/shard_map/while/body/eval_jaxpr/dot_general | solution.py:27
  234.5 8.6 %fusion.28 = f32[256]{0:T(256)S(1)} fusion(f32[256,448]{0,1:T(8,128)S(1)} %get-tuple-element.124, bf16[256,8192]{1,0:T(8,128)(2,1)} %get-tuple-element.123, bf16[448,8192]{1,0:T(8,128)(2,1)} %get-tuple-element.122, bf16[4,32,8192]{2,1,0:T(8,128)(2,1)} %get-tuple-element.121, s32[]{:T(128)} %get-tuple-element.109, ...), kind=kOutput, calls=%fused_computation.4.clone.1 | convolution fusion | flops 2128838400 | bytes 12552192 | tf_op jit(solution)/shard_map/while/body/eval_jaxpr/dot_general | solution.py:27
  243.1 62.3 %psum.7 = f32[256,4]{0,1:T(4,128)S(1)} all-reduce(f32[256,4]{0,1:T(4,128)S(1)} %bitcast.32), channel_id=1, replica_groups=mesh['grp'=4,'eig'=32] {'eig'}, use_global_device_ids=true, to_apply=%region_3.4 | all-reduce | flops 1024 | bytes 8192 | tf_op jit(solution)/shard_map/psum | solution.py:33
  305.4 9.5 %all_gather.19 = f32[1024,4]{0,1:T(4,128)S(1)} all-gather(f32[256,4]{0,1:T(4,128)S(1)} %psum.7), channel_id=1, replica_groups=mesh['grp'=4,'eig'=32] {'grp'}, dimensions={0}, use_global_device_ids=true | all-gather | bytes 20480 | tf_op jit(solution)/shard_map/all_gather | solution.py:34
  314.9 0.6 copy.16
  (5 shorter events, 0.2 us)
Async XLA Ops:
  6.5 52.7 %all-gather.7.cloned.1.call-start = ((), (), s32[]{:S(2)}) async-start(), calls=%async_computation.1 | async-start | bytes 4325376 | tf_op jit(solution)/shard_map/all_gather | solution.py:14
  7.3 104.4 %all-gather.11.cloned.1.call-start = ((), (), s32[]{:S(2)}) async-start(), calls=%async_computation.3 | async-start | bytes 7569408 | tf_op jit(solution)/shard_map/all_gather | solution.py:9
  8.0 149.8 %all-gather.5.cloned.1.call-start = ((), (), s32[]{:S(2)}) async-start(), calls=%async_computation | async-start | bytes 2162688 | tf_op jit(solution)/shard_map/all_gather | solution.py:19
  8.7 199.7 %all-gather.9.cloned.1.call-start = ((), (), s32[]{:S(2)}) async-start(), calls=%async_computation.2 | async-start | bytes 4325376 | tf_op jit(solution)/shard_map/all_gather | solution.py:18
Sparse Core Ops, SparseCore 0:
  9.6 49.5 all-gather.6
  61.5 50.1 all-gather.10
  113.8 43.8 all-gather.4
  159.8 48.5 all-gather.8
where the time goes:
time: 327 us; the launch traced here: 322 us
  waiting for transfers between devices  187 us (57%)
  blocking collectives  71.8 us (22%)
  matrix products  49.5 us (15%)
  between operations  13.1 us (4%)
    psum x1, blocking collectives, per_device(): summed = lax.psum(partial_scores, 'eig')  62.3 us
    all_gather x1, waiting for transfers between devices, per_device(): act_rot = lax.all_gather(act_local, 'eig', axis=1, tiled=True)  50.6 us
    all_gather x1, waiting for transfers between devices, per_device(): lax.all_gather(activations, 'eig', axis=0, tiled=True)  50.4 us
    all_gather x1, waiting for transfers between devices, per_device(): lax.all_gather(out_grads, 'eig', axis=0, tiled=True)  47 us
    all_gather x1, waiting for transfers between devices, per_device(): right_full = lax.all_gather(query_right, 'eig', axis=2, tiled=True)  36.5 us
    dot_general x4, matrix products, one_query(): lax.dot_general(act_rot, precond, (((1,), (1,)), ((), ())), preferred_ele...  34.5 us
    dot_general x1, matrix products, per_device(): jnp.dot(lax.all_gather(out_grads, 'eig', axis=0, tiled=True), grad_basis,...  9.58 us
    all_gather x1, blocking collectives, per_device(): return lax.all_gather(summed, 'grp', axis=0, tiled=True)  9.51 us
  transfers between devices with their start and end apart: 4, of which 4 were waited for; matrix products, arithmetic and copies ran while one was open for 5% of the time, Pallas kernels for 0%

commit v1 on v0

v1 whole, which is shorter than its diff:
```python
import jax
import jax.numpy as jnp
from jax import lax
from jax.experimental import pallas as pl
from jax.experimental.pallas import tpu as pltpu
from jax.sharding import PartitionSpec as P

MESH = pl.DeviceIdType.MESH
F32, BF16 = jnp.float32, jnp.bfloat16

FF, D, Q, R, T = 14336, 8192, 4, 32, 1024
EIG, GRP = 32, 4
ROWS = T // (EIG * GRP)
TG = T // GRP
FL, DL = FF // EIG, D // EIG
KP = D // 8
KA = D // 2
KG = FF // 2
NG = 4
KC = KG // NG
QI = Q * FL
NSEM = 112

NT = (((1,), (1,)), ((), ()))


def body(
    a_hbm, g_hbm, bt_hbm, ab_hbm, corr_hbm, ql_hbm, qr_hbm, out_ref,
    a_in, g_in, abuf, gbuf, rbuf, arbuf, pbuf, bt_v, corr_v, ql_v, lbd, inv_v,
    act_v, gr_v, acc_v, red1, red2, ssem, rsem, lsem,
):
    e = lax.axis_index("eig")
    z = lax.axis_index("grp")
    c, x, y = lax.rem(e, 2), lax.rem(e // 2, 4), e // 8
    s1, s2 = 2 + 6 * c, 8 - 6 * c
    p1, p2 = x + c * (y - x), y + c * (x - y)
    mod4 = lambda v: lax.rem(v + 4, 4)
    d1 = lambda k: {"eig": c + mod4(p1 + k) * s1 + p2 * s2}
    d2 = lambda k: {"eig": c + p1 * s1 + mod4(p2 + k) * s2}
    dz = lambda k: {"grp": mod4(z + k)}
    sib = {"eig": e + 1 - 2 * c}

    tags, sent = {}, []

    def send(tag, src, dst, dev):
        i = tags.setdefault(tag, len(tags))
        cp = pltpu.make_async_remote_copy(
            src_ref=src, dst_ref=dst, send_sem=ssem.at[i], recv_sem=rsem.at[i],
            device_id=dev, device_id_type=MESH)
        cp.start()
        sent.append(cp)

    def recv(tag, ref):
        pltpu.make_async_copy(ref, ref, rsem.at[tags[tag]]).wait()

    def local(i, src, dst):
        return pltpu.make_async_copy(src, dst, lsem.at[i])

    ld_a = local(0, a_hbm.at[:, pl.ds(pl.multiple_of(c * KA, KA), KA)], a_in.at[c])
    ld_g = local(1, g_hbm.at[:, pl.ds(pl.multiple_of(c * KG, KG), KG)], g_in.at[c])
    ld_r = local(2, qr_hbm.at[z], rbuf.at[c, z, p2, p1])
    ld_ql = local(3, ql_hbm, ql_v)

    ld_ab = [local(15 + i, ab_hbm.at[pl.ds(i * KP, KP)], pbuf.at[6 + i // 4, i % 4, pl.ds(0, KP)])
             for i in range(8)]

    def ld_bt(k, cc):
        at = cc * KG + k * KC
        return local(5 + cc, bt_hbm.at[:, pl.ds(at, KC)], bt_v.at[cc])

    def ld_corr(n, b):
        cc, row = n // 4, lax.rem(n, 4)
        eig = cc + b * (2 + 6 * cc) + row * (8 - 6 * cc)
        slot = lax.rem(n, 2)
        return local(7 + slot * 4 + b, corr_hbm.at[:, pl.ds(pl.multiple_of(eig * DL, DL), DL)],
                     corr_v.at[slot, b])

    for cp in (ld_a, ld_g, ld_r, ld_ql, *ld_ab):
        cp.start()
    for cc in range(2):
        ld_bt(0, cc).start()
    for b in range(4):
        ld_corr(0, b).start()

    barrier = pltpu.get_barrier_semaphore()
    for dev in [d1(1), d1(2), d1(3), d2(1), d2(2), d2(3), dz(1), dz(2), dz(3), sib]:
        pl.semaphore_signal(barrier, inc=1, device_id=dev, device_id_type=MESH)
    pl.semaphore_wait(barrier, 10)

    def p1_start(nm, whole):
        send(nm + "1+", whole(p1), whole(p1), d1(1))
        send(nm + "1-", whole(p1), whole(p1), d1(3))

    def p1_forward(nm, whole, half):
        left, right = mod4(p1 + 3), mod4(p1 + 1)
        recv(nm + "1+", whole(left))
        send(nm + "1f+", half(left, 0), half(left, 0), d1(1))
        recv(nm + "1-", whole(right))
        send(nm + "1f-", half(right, 1), half(right, 1), d1(3))

    def p1_end(nm, half):
        far = mod4(p1 + 2)
        recv(nm + "1f+", half(far, 0))
        recv(nm + "1f-", half(far, 1))

    def p2_start(nm, half):
        for tag, h, k in (("a+", 0, 1), ("a-", 1, 3), ("b+", 1, 1), ("b-", 0, 3)):
            send(nm + tag, half(p2, h), half(p2, h), d2(k))

    def p2_forward(nm, half):
        left, right = mod4(p2 + 3), mod4(p2 + 1)
        recv(nm + "a+", half(left, 0))
        send(nm + "2f+", half(left, 0), half(left, 0), d2(1))
        recv(nm + "a-", half(right, 1))
        send(nm + "2f-", half(right, 1), half(right, 1), d2(3))

    def p2_middle(nm, half):
        recv(nm + "b+", half(mod4(p2 + 3), 1))
        recv(nm + "b-", half(mod4(p2 + 1), 0))

    def p2_end(nm, half):
        far = mod4(p2 + 2)
        recv(nm + "2f+", half(far, 0))
        recv(nm + "2f-", half(far, 1))

    def share(nm, ref):
        send(nm, ref, ref, sib)

    a1 = lambda at: abuf.at[c, p2, at]
    a1h = lambda at, h: abuf.at[c, p2, at, :, pl.ds(h * (KA // 2), KA // 2)]
    a2h = lambda row, h: abuf.at[c, row, pl.ds(2 * h, 2)]
    g1 = lambda at: gbuf.at[c, :, p2, at]
    g1h = lambda at, h: gbuf.at[c, pl.ds(h * (NG // 2), NG // 2), p2, at]
    g2h = lambda k: lambda row, h: gbuf.at[c, k, row, pl.ds(2 * h, 2)]
    ar1 = lambda at: arbuf.at[c, p2, at]
    ar1h = lambda at, h: arbuf.at[c, p2, at, pl.ds(h * (TG // 2), TG // 2)]
    ar2h = lambda row, h: arbuf.at[c, row, pl.ds(2 * h, 2)]

    other = 1 - c
    send("sa", a_hbm.at[:, pl.ds(pl.multiple_of(other * KA, KA), KA)], a_in.at[c], sib)
    for k in (1, 3, 2):
        send(f"r1{k}", qr_hbm.at[z], rbuf.at[c, z, p2, p1], d1(k))
    send("sg", g_hbm.at[:, pl.ds(pl.multiple_of(other * KG, KG), KG)], g_in.at[c], sib)

    ld_a.wait()
    recv("sa", a_in.at[other])
    abuf[c, p2, p1] = jnp.concatenate([a_in[0].astype(F32), a_in[1].astype(F32)], axis=0).astype(BF16)
    p1_start("a", a1)
    ld_g.wait()
    recv("sg", g_in.at[other])
    for k in range(NG):
        cols = slice(k * KC, (k + 1) * KC)
        gbuf[c, k, p2, p1] = jnp.concatenate(
            [g_in[0, :, cols].astype(F32), g_in[1, :, cols].astype(F32)], axis=0).astype(BF16)
    p1_start("g", g1)

    ld_r.wait()
    for k in (1, 3, 2):
        recv(f"r1{k}", rbuf.at[c, z, p2, mod4(p1 - k)])
    for k in (1, 3, 2):
        send(f"r2{k}", rbuf.at[c, z, p2], rbuf.at[c, z, p2], d2(k))
    p1_forward("a", a1, a1h)

    ld_ql.wait()
    lt = ql_v[...].reshape(Q * R, FL).astype(F32)
    lt = jnp.concatenate([lt, jnp.zeros((Q * R, 512 - FL), F32)], axis=1).T[:FL]
    lane = lax.broadcasted_iota(jnp.int32, (FL, Q * R), 1)
    for q in range(Q):
        keep = (lane >= q * R) & (lane < (q + 1) * R)
        lbd[q * FL:(q + 1) * FL] = jnp.where(keep, lt, 0.0).astype(BF16)

    for k in (1, 3, 2):
        recv(f"r2{k}", rbuf.at[c, z, mod4(p2 - k)])
    for k in (1, 3, 2):
        send(f"rz{k}", rbuf.at[c, z], rbuf.at[c, z], dz(k))
    share("rs0", rbuf.at[c, z])

    p1_end("a", a1h)
    p2_start("a", a2h)
    share("as0", abuf.at[c, p2])
    p1_forward("g", g1, g1h)
    p1_end("g", g1h)
    p2_forward("a", a2h)
    p2_start("g0", g2h(0))
    p2_middle("a", a2h)
    share("as1", abuf.at[c, mod4(p2 + 1)])
    share("as3", abuf.at[c, mod4(p2 + 3)])
    p2_end("a", a2h)
    share("as2", abuf.at[c, mod4(p2 + 2)])
    p2_forward("g0", g2h(0))
    p2_start("g1", g2h(1))
    for k in (1, 3, 2):
        recv(f"rz{k}", rbuf.at[c, mod4(z - k)])
        share(f"rs{k}", rbuf.at[c, mod4(z - k)])

    for cp in ld_ab:
        cp.wait()
    for k in range(4):
        recv(f"as{k}", abuf.at[other, mod4(p1 + k)])
    for cc in range(2):
        for piece in range(4):
            cols = slice(piece * KP, (piece + 1) * KP)
            av = abuf[cc, :, :, :, cols]
            if cc == 1:
                av = jnp.swapaxes(av, 0, 1)
            part = jnp.dot(av.reshape(TG, KP), pbuf[6 + cc, piece, :KP], preferred_element_type=F32)
            if cc == 0 and piece == 0:
                act_v[...] = part
            else:
                act_v[...] += part
    arbuf[c, p2, p1] = act_v[...].astype(BF16)
    p1_start("r", ar1)

    for k in range(4):
        recv(f"rs{k}", rbuf.at[other, mod4(z - k)])

    def precond(n):
        cc, row = n // 4, lax.rem(n, 4)
        slot = lax.rem(n, 2)

        @pl.when(n < 7)
        def _():
            for b in range(4):
                ld_corr(n + 1, b).start()

        for b in range(4):
            ld_corr(n, b).wait()

        def one(b, _):
            inv_v[...] = 1.0 / (corr_v[slot, b].astype(F32) + 0.1)
            right = rbuf[cc, :, row, b].reshape(Q * R, DL)
            for q in range(Q):
                prod = jnp.dot(lbd[q * FL:(q + 1) * FL], right, preferred_element_type=F32)
                pbuf[n, b, q * FL:(q + 1) * FL] = (prod * inv_v[...]).astype(BF16)
            return 0

        lax.fori_loop(0, 4, one, 0)

    def preconds(lo, hi):
        lax.fori_loop(lo, hi, lambda n, _: (precond(n), 0)[1], 0)

    def grad_chunk(k):
        recv(f"gs{k}", gbuf.at[other, k])
        for cc in range(2):
            ld_bt(k, cc).wait()
            gv = gbuf[cc, k]
            if cc == 1:
                gv = jnp.swapaxes(gv, 0, 1)
            part = lax.dot_general(bt_v[cc], gv.reshape(TG, KC), NT, preferred_element_type=F32)
            if k == 0 and cc == 0:
                gr_v[...] = part
            else:
                gr_v[...] += part
            if k + 1 < NG:
                ld_bt(k + 1, cc).start()

    preconds(0, 1)
    p2_middle("g0", g2h(0))
    p2_end("g0", g2h(0))
    share("gs0", gbuf.at[c, 0])
    p2_forward("g1", g2h(1))
    p2_start("g2", g2h(2))
    p1_forward("r", ar1, ar1h)
    preconds(1, 2)
    p1_end("r", ar1h)
    share("rr0", arbuf.at[c, p2])
    p2_middle("g1", g2h(1))
    p2_end("g1", g2h(1))
    share("gs1", gbuf.at[c, 1])
    p2_forward("g2", g2h(2))
    p2_start("g3", g2h(3))
    grad_chunk(0)
    preconds(2, 4)
    p2_middle("g2", g2h(2))
    p2_end("g2", g2h(2))
    share("gs2", gbuf.at[c, 2])
    p2_forward("g3", g2h(3))
    p2_start("r", ar2h)
    grad_chunk(1)
    preconds(4, 5)
    p2_middle("g3", g2h(3))
    p2_end("g3", g2h(3))
    share("gs3", gbuf.at[c, 3])
    p2_forward("r", ar2h)
    grad_chunk(2)
    preconds(5, 8)
    grad_chunk(3)

    def applied(cc, row, first=False):
        n = cc * 4 + row
        rhs = jnp.concatenate([arbuf[cc, row, b] for b in range(4)], axis=1)

        def tile(m, _):
            rows = pl.ds(pl.multiple_of(m * FL, FL), FL)
            lhs = jnp.concatenate([pbuf[n, b, rows] for b in range(4)], axis=1)
            part = lax.dot_general(lhs, rhs, NT, preferred_element_type=F32)
            if first:
                acc_v[rows] = part
            else:
                acc_v[rows] += part
            return 0

        lax.fori_loop(0, Q, tile, 0)

    applied(c, p2, True)
    recv("rr0", arbuf.at[other, p1])
    p2_middle("r", ar2h)
    share("rr1", arbuf.at[c, mod4(p2 + 1)])
    share("rr3", arbuf.at[c, mod4(p2 + 3)])
    applied(other, p1)
    applied(c, mod4(p2 + 1))
    applied(c, mod4(p2 + 3))
    p2_end("r", ar2h)
    share("rr2", arbuf.at[c, mod4(p2 + 2)])
    for k in (1, 3):
        recv(f"rr{k}", arbuf.at[other, mod4(p1 + k)])
        applied(other, mod4(p1 + k))
    applied(c, mod4(p2 + 2))
    recv("rr2", arbuf.at[other, mod4(p1 + 2)])
    applied(other, mod4(p1 + 2))

    gr = gr_v[...]
    sc = [jnp.sum(acc_v[q * FL:(q + 1) * FL] * gr, axis=0, keepdims=True) for q in range(Q)]
    sc = jnp.concatenate(sc, axis=0)
    place1 = x * 2 + c
    red1[place1] = jnp.concatenate([sc[:, :128], sc[:, 128:]], axis=0)
    for k in range(1, 8):
        to = lax.rem(place1 + k, 8)
        send(f"s1{k}", red1.at[place1], red1.at[place1], {"eig": y * 8 + to})
    for k in range(1, 8):
        recv(f"s1{k}", red1.at[lax.rem(place1 + 8 - k, 8)])
    red2[z, y] = jnp.sum(red1[...], axis=0)
    for kz in range(4):
        for ky in range(4):
            if kz or ky:
                send(f"s2{kz}{ky}", red2.at[z, y], red2.at[z, y],
                     {"grp": mod4(z + kz), "eig": mod4(y + ky) * 8 + place1})
    for kz in range(4):
        for ky in range(4):
            if kz or ky:
                recv(f"s2{kz}{ky}", red2.at[mod4(z - kz), mod4(y - ky)])
    for g in range(GRP):
        total = jnp.sum(red2[g], axis=0)
        for half in range(2):
            out_ref[:, g * TG + half * 128:g * TG + (half + 1) * 128] = total[half * 4:half * 4 + 4]
    for cp in sent:
        cp.wait_send()
    assert len(tags) <= NSEM, len(tags)


def per_device(out_grads, activations, grad_basis, act_basis, corrections, query_left, query_right):
    any_, vmem = pl.BlockSpec(memory_space=pl.ANY), pl.BlockSpec(memory_space=pltpu.VMEM)
    out = pl.pallas_call(
        body,
        out_shape=jax.ShapeDtypeStruct((Q, T), F32),
        in_specs=[any_] * 7,
        out_specs=vmem,
        scratch_shapes=[
            pltpu.VMEM((2, ROWS, KA), BF16),
            pltpu.VMEM((2, ROWS, KG), BF16),
            pltpu.VMEM((2, 4, 4, 16, KA), BF16),
            pltpu.VMEM((2, NG, 4, 4, 16, KC), BF16),
            pltpu.VMEM((2, Q, 4, 4, R, DL), BF16),
            pltpu.VMEM((2, 4, 4, TG, DL), BF16),
            pltpu.VMEM((8, 4, QI, DL), BF16),
            pltpu.VMEM((2, FL, KC), BF16),
            pltpu.VMEM((2, 4, FL, DL), BF16),
            pltpu.VMEM((Q, R, FL), BF16),
            pltpu.VMEM((QI, Q * R), BF16),
            pltpu.VMEM((FL, DL), F32),
            pltpu.VMEM((TG, DL), F32),
            pltpu.VMEM((FL, TG), F32),
            pltpu.VMEM((QI, TG), F32),
            pltpu.VMEM((8, 8, 128), F32),
            pltpu.VMEM((GRP, 4, 8, 128), F32),
            pltpu.SemaphoreType.DMA((NSEM,)),
            pltpu.SemaphoreType.DMA((NSEM,)),
            pltpu.SemaphoreType.DMA((23,)),
        ],
        compiler_params=pltpu.CompilerParams(
            collective_id=0, has_side_effects=True, vmem_limit_bytes=60 * 1024 * 1024),
    )(activations, out_grads, grad_basis.T, act_basis, corrections, query_left, query_right)
    return out.T


def solution(mesh):
    placed = (
        P(("grp", "eig"), None),
        P(("grp", "eig"), None),
        P(None, "eig"),
        P(None, "eig"),
        P("eig", None),
        P(None, None, "eig"),
        P(None, None, "eig"),
    )
    return jax.shard_map(per_device, mesh=mesh, in_specs=placed, out_specs=P(), check_vma=False)
```

time: 327 us -> 90.8 us (0.28); the launches traced: 322 us -> 90.6 us
  waiting for transfers between devices: 187 us -> 0 us
  Pallas kernels: 0 us -> 89.3 us
  blocking collectives: 71.8 us -> 0 us
  matrix products: 49.5 us -> 0 us
  between operations: 13.1 us -> 0.01 us
    all_gather x4 -> x0, waiting for transfers between devices: 185 us -> none  [the longest x1 50.6 us: per_device(): act_rot = lax.all_gather(act_local, 'eig', axis=1, tiled=True)]
    pallas_call x0 -> x1, Pallas kernels: none -> 89.3 us  [per_device(): pl.pallas_call(body, out_shape=jax.ShapeDtypeStruct((Q, T), F32), in_spec...]
    psum x1 -> x0, blocking collectives: 62.3 us -> none  [per_device(): summed = lax.psum(partial_scores, 'eig')]
    dot_general x6 -> x0, matrix products: 49.5 us -> none  [the longest x4 34.5 us: one_query(): lax.dot_general(act_rot, precond, (((1,), (1,)), ((), ())), preferred_ele...]
    all_gather x1 -> x0, blocking collectives: 9.51 us -> none  [per_device(): return lax.all_gather(summed, 'grp', axis=0, tiled=True)]
  transfers between devices with their start and end apart: 4 -> 0, of which waited for: 4 -> 0; matrix products, arithmetic and copies ran while one was open for 5% -> 0% of each run, Pallas kernels for 0% -> 0%
where the time goes in v1:
time: 90.8 us; the launch traced here: 90.6 us
  Pallas kernels  89.3 us (98%)
  local copies, waits for them, and re-layouts  1.32 us (1%)
    pallas_call x1, Pallas kernels, per_device(): pl.pallas_call(body, out_shape=jax.ShapeDtypeStruct((Q, T), F32), in_spec...  89.3 us

profile of v1, /device:TPU:1, one launch (start us, length us, event | category | flops | bytes accessed | tf_op | source)
XLA Modules:
  0.0 90.6 jit_solution(7547438535114970618)
XLA Ops:
  0.0 89.3 %shard_map.73 = f32[4,1024]{1,0:T(4,128)} custom-call(bf16[8,8192]{1,0:T(8,128)(2,1)} %a_hbm.1, bf16[8,14336]{1,0:T(8,128)(2,1)} %g_hbm.1, bf16[448,14336]{1,0:T(8,128)(2,1)} %bitcast.2, bf16[8192,256]{1,0:T(8,128)(2,1)} %ab_hbm.1, bf16[448,8192]{1,0:T(8,128)(2,1)} %corr_hbm.1, bf16[4,32,448]{2,1,0:T(8,128)(2,1)} %ql_hbm.1, bf16[4,32,256]{2,1,0:T(8,128)(2,1)} %qr_hbm.1), custom_call_target="tpu_custom_call" | custom-call | tf_op jit(solution)/shard_map/pallas_call | solution.py:353
  89.3 1.3 %copy.9 = f32[1024,4]{0,1:T(4,128)} copy(f32[1024,4]{0,1:T(4,128)} %bitcast.3) | data formatting | bytes 32768

commit v2 on v0

v2 whole, which is shorter than its diff:
```python
import jax
import jax.numpy as jnp
from jax import lax
from jax.experimental import pallas as pl
from jax.experimental.pallas import tpu as pltpu
from jax.sharding import PartitionSpec as P

MESH = pl.DeviceIdType.MESH
F32, BF16 = jnp.float32, jnp.bfloat16

FF, D, Q, R, T = 14336, 8192, 4, 32, 1024
EIG, GRP = 32, 4
ROWS = T // (EIG * GRP)
TG = T // GRP
FL, DL = FF // EIG, D // EIG
KP = D // 8
KA = D // 2
KG = FF // 2
NG = 2
KC = KG // NG
KB = KC // 2
QI = Q * FL
QP = 2 * FL
NSEM = 120

NT = (((1,), (1,)), ((), ()))


def body(
    a_hbm, g_hbm, bt_hbm, ab_hbm, corr_hbm, ql_hbm, qr_hbm, out_ref,
    a_in, g_in, abuf, gbuf, rbuf, arbuf, pbuf, bt_v, ab_v, ql_v, lbd, inv_v,
    act_v, gr_v, acc_v, red1, red2, ssem, rsem, lsem,
):
    e = lax.axis_index("eig")
    z = lax.axis_index("grp")
    c, x, y = lax.rem(e, 2), lax.rem(e // 2, 4), e // 8
    s1, s2 = 2 + 6 * c, 8 - 6 * c
    p1, p2 = x + c * (y - x), y + c * (x - y)
    mod4 = lambda v: lax.rem(v + 4, 4)
    d1 = lambda k: {"eig": c + mod4(p1 + k) * s1 + p2 * s2}
    d2 = lambda k: {"eig": c + p1 * s1 + mod4(p2 + k) * s2}
    dz = lambda k: {"grp": mod4(z + k)}
    sib = {"eig": e + 1 - 2 * c}

    tags, sent = {}, []

    def send(tag, src, dst, dev):
        i = tags.setdefault(tag, len(tags))
        cp = pltpu.make_async_remote_copy(
            src_ref=src, dst_ref=dst, send_sem=ssem.at[i], recv_sem=rsem.at[i],
            device_id=dev, device_id_type=MESH)
        cp.start()
        sent.append(cp)

    def recv(tag, ref):
        pltpu.make_async_copy(ref, ref, rsem.at[tags[tag]]).wait()

    def local(i, src, dst):
        return pltpu.make_async_copy(src, dst, lsem.at[i])

    ld_a = local(0, a_hbm.at[:, pl.ds(pl.multiple_of(c * KA, KA), KA)], a_in.at[c])
    ld_g = local(1, g_hbm.at[:, pl.ds(pl.multiple_of(c * KG, KG), KG)], g_in.at[c])
    pair = lax.rem(z, 2)
    r_own = qr_hbm.at[pl.ds(2 * pair, 2)]
    ld_r = local(2, r_own, rbuf.at[c, pair, p2, p1])
    ld_ql = local(3, ql_hbm, ql_v)

    def ld_ab(i):
        return local(7 + i % 4, ab_hbm.at[pl.ds(i * KP, KP)], ab_v.at[i % 4])

    def ld_bt(i):
        k, cc, h = i // 4, i // 2 % 2, i % 2
        return local(5 + i % 2, bt_hbm.at[:, pl.ds(cc * KG + k * KC + h * KB, KB)], bt_v.at[i % 2])

    def ld_corr(n, b):
        cc, row = n // 4, lax.rem(n, 4)
        eig = cc + b * (2 + 6 * cc) + row * (8 - 6 * cc)
        return local(11 + n * 4 + b, corr_hbm.at[:, pl.ds(pl.multiple_of(eig * DL, DL), DL)],
                     pbuf.at[n, b, pl.ds(pl.multiple_of((1 - pair) * QP, QP), FL)])

    for cp in (ld_a, ld_g, ld_r, ld_ql):
        cp.start()
    for i in range(4):
        ld_ab(i).start()
    for i in range(2):
        ld_bt(i).start()

    def start_corr(n, _):
        for b in range(4):
            ld_corr(n, b).start()
        return 0

    lax.fori_loop(0, 8, start_corr, 0)

    barrier = pltpu.get_barrier_semaphore()
    for dev in [d1(1), d1(2), d1(3), d2(1), d2(2), d2(3), dz(1), dz(2), dz(3), sib]:
        pl.semaphore_signal(barrier, inc=1, device_id=dev, device_id_type=MESH)
    pl.semaphore_wait(barrier, 10)

    left1, right1, far1 = mod4(p1 + 3), mod4(p1 + 1), mod4(p1 + 2)
    left2, right2, far2 = mod4(p2 + 3), mod4(p2 + 1), mod4(p2 + 2)
    place = {"o": p1, "l": left1, "r": right1, "f": far1}

    class Gather:
        def __init__(self, nm, blk, half):
            self.nm, self.blk, self.half = nm, blk, half

        def _send(self, tag, ref, dev):
            send(self.nm + tag, ref, ref, dev)

        def first(self):
            own = self.blk(p2, p1)
            self._send("1+", own, d1(1))
            self._send("1-", own, d1(3))

        def first_forward(self, b):
            if b == "l":
                recv(self.nm + "1+", self.blk(p2, left1))
                self._send("1f+", self.half(left1, 0), d1(1))
            else:
                recv(self.nm + "1-", self.blk(p2, right1))
                self._send("1f-", self.half(right1, 1), d1(3))

        def first_far(self):
            recv(self.nm + "1f+", self.half(far1, 0))
            recv(self.nm + "1f-", self.half(far1, 1))

        def second(self, b):
            ref = self.blk(p2, place[b])
            self._send("2+" + b, ref, d2(1))
            self._send("2-" + b, ref, d2(3))

        def forward(self, b):
            if b in "of":
                recv(self.nm + "2+" + b, self.blk(left2, place[b]))
                self._send("2f" + b, self.blk(left2, place[b]), d2(1))
            else:
                recv(self.nm + "2-" + b, self.blk(right2, place[b]))
                self._send("2f" + b, self.blk(right2, place[b]), d2(3))

        def share(self, k):
            self._send(f"s{k}", self.row(c, mod4(p2 + k)), sib)

        def near_row(self, b):
            if b == "l":
                recv(self.nm + "2+l", self.blk(left2, left1))
                recv(self.nm + "2+r", self.blk(left2, right1))
                self.share(3)
            else:
                recv(self.nm + "2-o", self.blk(right2, p1))
                recv(self.nm + "2-f", self.blk(right2, far1))
                self.share(1)

        def far_row(self):
            for b in "olrf":
                recv(self.nm + "2f" + b, self.blk(far2, place[b]))
            self.share(2)

        def shared(self, k):
            recv(f"{self.nm}s{k}", self.row(other, mod4(p1 + k)))

        def all_shared(self):
            for k in range(4):
                self.shared(k)

    other = 1 - c
    ga = Gather("a", lambda row, at: abuf.at[c, row, at],
                lambda at, h: abuf.at[c, p2, at, :, pl.ds(h * (KA // 2), KA // 2)])
    ga.row = lambda cc, row: abuf.at[cc, row]

    def gather_g(k):
        g = Gather(f"g{k}", lambda row, at: gbuf.at[c, k, row, at],
                   lambda at, h: gbuf.at[c, k, p2, at, :, pl.ds(h * (KC // 2), KC // 2)])
        g.row = lambda cc, row: gbuf.at[cc, k, row]
        return g

    g0, g1 = gather_g(0), gather_g(1)
    gt = Gather("t", lambda row, at: arbuf.at[c, row, at],
                 lambda at, h: arbuf.at[c, p2, at, pl.ds(h * (TG // 2), TG // 2)])
    gt.row = lambda cc, row: arbuf.at[cc, row]

    def act_rot():
        ga.all_shared()
        for i in range(8):
            cc = i // 4
            ld_ab(i).wait()
            av = abuf[cc, :, :, :, i % 4 * KP:(i % 4 + 1) * KP]
            if cc == 1:
                av = jnp.swapaxes(av, 0, 1)
            part = jnp.dot(av.reshape(TG, KP), ab_v[i % 4], preferred_element_type=F32)
            if i == 0:
                act_v[...] = part
            else:
                act_v[...] += part
            if i < 4:
                ld_ab(i + 4).start()
        arbuf[c, p2, p1] = act_v[...].astype(BF16)

    def precond(second, n):
        at = 1 - pair if second else pair
        cc, row = n // 4, lax.rem(n, 4)
        if not second:
            for b in range(4):
                ld_corr(n, b).wait()

        def one(b, _):
            corr = pbuf[n, b, pl.ds(pl.multiple_of((1 - pair) * QP, QP), FL)]
            inv_v[...] = 1.0 / (corr.astype(F32) + 0.1)
            right = rbuf[cc, at, row, b].reshape(2 * R, DL)
            for q in range(2):
                prod = jnp.dot(lbd[at, q * FL:(q + 1) * FL], right, preferred_element_type=F32)
                pbuf[n, b, pl.ds(pl.multiple_of(at * QP + q * FL, FL), FL)] = (prod * inv_v[...]).astype(BF16)
            return 0

        lax.fori_loop(0, 4, one, 0)

    def preconds(second, lo, hi):
        lax.fori_loop(lo, hi, lambda n, _: (precond(second, n), 0)[1], 0)

    def grad_piece(i):
        k, cc, h = i // 4, i // 2 % 2, i % 2
        ld_bt(i).wait()
        gv = gbuf[cc, k, :, :, :, h * KB:(h + 1) * KB]
        if cc == 1:
            gv = jnp.swapaxes(gv, 0, 1)
        part = lax.dot_general(bt_v[i % 2], gv.reshape(TG, KB), NT, preferred_element_type=F32)
        if i == 0:
            gr_v[...] = part
        else:
            gr_v[...] += part
        if i + 2 < 8:
            ld_bt(i + 2).start()

    def applied(groups):
        def group(i, _):
            cc, row = groups[0]
            for at, (cc_at, row_at) in enumerate(groups):
                cc, row = jnp.where(i == at, cc_at, cc), jnp.where(i == at, row_at, row)
            rhs = jnp.concatenate([arbuf[cc, row, b] for b in range(4)], axis=1)
            for m in range(7):
                rows = slice(m * 256, (m + 1) * 256)
                lhs = jnp.concatenate([pbuf[cc * 4 + row, b, rows] for b in range(4)], axis=1)
                acc_v[rows] += lax.dot_general(lhs, rhs, NT, preferred_element_type=F32)
            return 0

        lax.fori_loop(0, len(groups), group, 0)

    def share_pair(k):
        ref = rbuf.at[c, 1 - pair, :, :, k // 2]
        recv(f"rz{k}", ref)
        send(f"rs{k}", ref, ref, sib)

    def left_factors():
        ld_ql.wait()
        for at in range(2):
            lt = ql_v[2 * at:2 * at + 2].reshape(2 * R, FL).astype(F32)
            lt = jnp.concatenate([lt, jnp.zeros((2 * R, 512 - FL), F32)], axis=1)
            lt = jnp.concatenate([lt, jnp.zeros((2 * R, 512), F32)], axis=0).T[:FL]
            lane = lax.broadcasted_iota(jnp.int32, (FL, 4 * R), 1)
            for q in range(2):
                keep = (lane >= q * R) & (lane < (q + 1) * R)
                lbd[at, q * FL:(q + 1) * FL] = jnp.where(keep, lt, 0.0)[:, :2 * R].astype(BF16)

        acc_v[...] = jnp.zeros_like(acc_v)

    def own_activations():
        ld_a.wait()
        recv("sa", a_in.at[other])
        abuf[c, p2, p1] = jnp.concatenate([a_in[0].astype(F32), a_in[1].astype(F32)], axis=0).astype(BF16)

    def own_out_grads():
        ld_g.wait()
        recv("sg", g_in.at[other])
        for k in range(NG):
            cols = slice(k * KC, (k + 1) * KC)
            gbuf[c, k, p2, p1] = jnp.concatenate(
                [g_in[0, :, cols].astype(F32), g_in[1, :, cols].astype(F32)], axis=0).astype(BF16)

    def right_rows():
        ld_r.wait()
        for k in (1, 3, 2):
            recv(f"r1{k}", rbuf.at[c, pair, p2, mod4(p1 - k)])
        for k in (1, 3, 2):
            send(f"r2{k}", rbuf.at[c, pair, p2], rbuf.at[c, pair, p2], d2(k))

    def right_along_z():
        for k in (1, 3, 2):
            recv(f"r2{k}", rbuf.at[c, pair, mod4(p2 - k)])
        for k in (1, 3):
            ref = rbuf.at[c, pair, :, :, k // 2]
            send(f"rz{k}", ref, ref, dz(k))
        send("rs0", rbuf.at[c, pair], rbuf.at[c, pair], sib)

    send("sa", a_hbm.at[:, pl.ds(pl.multiple_of(other * KA, KA), KA)], a_in.at[c], sib)
    for k in (1, 3, 2):
        send(f"r1{k}", r_own, rbuf.at[c, pair, p2, p1], d1(k))
    send("sg", g_hbm.at[:, pl.ds(pl.multiple_of(other * KG, KG), KG)], g_in.at[c], sib)
    left_factors()
    own_activations()
    ga.first()
    own_out_grads()
    g0.first()
    right_rows()
    ga.second("o")
    ga.first_forward("r")
    ga.first_forward("l")
    ga.second("l")
    g0.first_forward("r")
    ga.first_far()
    ga.second("f")
    ga.share(0)
    g0.first_forward("l")
    ga.second("r")
    right_along_z()
    recv("rs0", rbuf.at[other, pair])
    preconds(False, 0, 2)
    ga.forward("o")
    ga.forward("l")
    g1.first()
    ga.forward("r")
    ga.forward("f")
    ga.near_row("l")
    g0.second("l")
    g0.first_far()
    g0.second("f")
    g0.second("r")
    preconds(False, 2, 4)
    share_pair(1)
    g0.second("o")
    share_pair(3)
    g1.first_forward("l")
    g1.second("l")
    g1.first_forward("r")
    g1.second("o")
    g1.second("r")
    ga.near_row("r")
    ga.far_row()
    for k in (1, 3):
        recv(f"rs{k}", rbuf.at[other, 1 - pair, :, :, k // 2])
    preconds(False, 4, 6)
    g0.forward("l")
    act_rot()
    gt.second("o")
    g0.forward("r")
    gt.first()
    preconds(True, 0, 4)
    g0.forward("f")
    preconds(False, 6, 8)
    g0.forward("o")
    g0.near_row("r")
    g0.share(0)
    gt.first_forward("r")
    gt.first_forward("l")
    g0.near_row("l")
    g1.first_far()
    g1.share(0)
    g1.second("f")
    preconds(True, 4, 6)
    gt.second("l")
    preconds(True, 6, 8)
    gt.first_far()
    gt.second("f")
    gt.second("r")
    g1.forward("l")
    g1.forward("o")
    g0.far_row()
    gt.share(0)
    applied([(c, p2)])
    g1.forward("r")
    g1.near_row("r")
    g0.all_shared()
    grad_piece(0)
    grad_piece(1)
    gt.shared(0)
    g1.forward("f")
    g1.near_row("l")
    gt.forward("o")
    gt.forward("l")
    applied([(other, p1)])
    grad_piece(2)
    grad_piece(3)
    gt.forward("f")
    gt.near_row("l")
    applied([(c, left2)])
    gt.forward("r")
    gt.near_row("r")
    applied([(c, right2)])
    g1.far_row()
    gt.shared(3)
    applied([(other, left1)])
    gt.shared(1)
    applied([(other, right1)])
    g1.all_shared()
    grad_piece(4)
    grad_piece(5)
    gt.far_row()
    applied([(c, far2)])
    grad_piece(6)
    grad_piece(7)
    gt.shared(2)
    applied([(other, far1)])

    gr = gr_v[...]
    sc = [jnp.sum(acc_v[q * FL:(q + 1) * FL] * gr, axis=0, keepdims=True) for q in range(Q)]
    sc = jnp.concatenate(sc, axis=0)
    place1 = x * 2 + c
    red1[place1] = jnp.concatenate([sc[:, :128], sc[:, 128:]], axis=0)
    for k in range(1, 8):
        to = lax.rem(place1 + k, 8)
        send(f"s1{k}", red1.at[place1], red1.at[place1], {"eig": y * 8 + to})
    for k in range(1, 8):
        recv(f"s1{k}", red1.at[lax.rem(place1 + 8 - k, 8)])
    red2[z, y] = jnp.sum(red1[...], axis=0)
    for kz in range(4):
        for ky in range(4):
            if kz or ky:
                send(f"s2{kz}{ky}", red2.at[z, y], red2.at[z, y],
                     {"grp": mod4(z + kz), "eig": mod4(y + ky) * 8 + place1})
    for kz in range(4):
        for ky in range(4):
            if kz or ky:
                recv(f"s2{kz}{ky}", red2.at[mod4(z - kz), mod4(y - ky)])
    for g in range(GRP):
        total = jnp.sum(red2[g], axis=0)
        for half in range(2):
            out_ref[:, g * TG + half * 128:g * TG + (half + 1) * 128] = total[half * 4:half * 4 + 4]
    for cp in sent:
        cp.wait_send()
    assert len(tags) <= NSEM, len(tags)


def per_device(out_grads, activations, grad_basis, act_basis, corrections, query_left, query_right):
    any_, vmem = pl.BlockSpec(memory_space=pl.ANY), pl.BlockSpec(memory_space=pltpu.VMEM)
    out = pl.pallas_call(
        body,
        out_shape=jax.ShapeDtypeStruct((Q, T), F32),
        in_specs=[any_] * 7,
        out_specs=vmem,
        scratch_shapes=[
            pltpu.VMEM((2, ROWS, KA), BF16),
            pltpu.VMEM((2, ROWS, KG), BF16),
            pltpu.VMEM((2, 4, 4, 16, KA), BF16),
            pltpu.VMEM((2, NG, 4, 4, 16, KC), BF16),
            pltpu.VMEM((2, 2, 4, 4, 2, R, DL), BF16),
            pltpu.VMEM((2, 4, 4, TG, DL), BF16),
            pltpu.VMEM((8, 4, QI, DL), BF16),
            pltpu.VMEM((2, FL, KB), BF16),
            pltpu.VMEM((4, KP, DL), BF16),
            pltpu.VMEM((Q, R, FL), BF16),
            pltpu.VMEM((2, QP, 2 * R), BF16),
            pltpu.VMEM((FL, DL), F32),
            pltpu.VMEM((TG, DL), F32),
            pltpu.VMEM((FL, TG), F32),
            pltpu.VMEM((QI, TG), F32),
            pltpu.VMEM((8, 8, 128), F32),
            pltpu.VMEM((GRP, 4, 8, 128), F32),
            pltpu.SemaphoreType.DMA((NSEM,)),
            pltpu.SemaphoreType.DMA((NSEM,)),
            pltpu.SemaphoreType.DMA((43,)),
        ],
        compiler_params=pltpu.CompilerParams(
            collective_id=0, has_side_effects=True, vmem_limit_bytes=60 * 1024 * 1024),
    )(activations, out_grads, grad_basis.T, act_basis, corrections, query_left, query_right)
    return out.T


def solution(mesh):
    placed = (
        P(("grp", "eig"), None),
        P(("grp", "eig"), None),
        P(None, "eig"),
        P(None, "eig"),
        P("eig", None),
        P(None, None, "eig"),
        P(None, None, "eig"),
    )
    return jax.shard_map(per_device, mesh=mesh, in_specs=placed, out_specs=P(), check_vma=False)
```

time: 327 us -> 75.3 us (0.23); the launches traced: 322 us -> 75.1 us
  waiting for transfers between devices: 187 us -> 0 us
  Pallas kernels: 0 us -> 73.8 us
  blocking collectives: 71.8 us -> 0 us
  matrix products: 49.5 us -> 0 us
  between operations: 13.1 us -> 0.01 us
    all_gather x4 -> x0, waiting for transfers between devices: 185 us -> none  [the longest x1 50.6 us: per_device(): act_rot = lax.all_gather(act_local, 'eig', axis=1, tiled=True)]
    pallas_call x0 -> x1, Pallas kernels: none -> 73.8 us  [per_device(): pl.pallas_call(body, out_shape=jax.ShapeDtypeStruct((Q, T), F32), in_spec...]
    psum x1 -> x0, blocking collectives: 62.3 us -> none  [per_device(): summed = lax.psum(partial_scores, 'eig')]
    dot_general x6 -> x0, matrix products: 49.5 us -> none  [the longest x4 34.5 us: one_query(): lax.dot_general(act_rot, precond, (((1,), (1,)), ((), ())), preferred_ele...]
    all_gather x1 -> x0, blocking collectives: 9.51 us -> none  [per_device(): return lax.all_gather(summed, 'grp', axis=0, tiled=True)]
  transfers between devices with their start and end apart: 4 -> 0, of which waited for: 4 -> 0; matrix products, arithmetic and copies ran while one was open for 5% -> 0% of each run, Pallas kernels for 0% -> 0%
where the time goes in v2:
time: 75.3 us; the launch traced here: 75.1 us
  Pallas kernels  73.8 us (98%)
  local copies, waits for them, and re-layouts  1.32 us (2%)
    pallas_call x1, Pallas kernels, per_device(): pl.pallas_call(body, out_shape=jax.ShapeDtypeStruct((Q, T), F32), in_spec...  73.8 us

profile of v2, /device:TPU:1, one launch (start us, length us, event | category | flops | bytes accessed | tf_op | source)
XLA Modules:
  0.0 75.1 jit_solution(4397765590450963190)
XLA Ops:
  0.0 73.8 %shard_map.73 = f32[4,1024]{1,0:T(4,128)} custom-call(bf16[8,8192]{1,0:T(8,128)(2,1)} %a_hbm.1, bf16[8,14336]{1,0:T(8,128)(2,1)} %g_hbm.1, bf16[448,14336]{1,0:T(8,128)(2,1)} %bitcast.2, bf16[8192,256]{1,0:T(8,128)(2,1)} %ab_hbm.1, bf16[448,8192]{1,0:T(8,128)(2,1)} %corr_hbm.1, bf16[4,32,448]{2,1,0:T(8,128)(2,1)} %ql_hbm.1, bf16[4,32,256]{2,1,0:T(8,128)(2,1)} %qr_hbm.1), custom_call_target="tpu_custom_call" | custom-call | tf_op jit(solution)/shard_map/pallas_call | solution.py:434
  73.8 1.3 %copy.9 = f32[1024,4]{0,1:T(4,128)} copy(f32[1024,4]{0,1:T(4,128)} %bitcast.3) | data formatting | bytes 32768

commit v3 on v2

--- a/solution.py
+++ b/solution.py
@@ -65,8 +65,9 @@
     ld_r = local(2, r_own, rbuf.at[c, pair, p2, p1])
     ld_ql = local(3, ql_hbm, ql_v)
 
-    def ld_ab(i):
-        return local(7 + i % 4, ab_hbm.at[pl.ds(i * KP, KP)], ab_v.at[i % 4])
+    def ld_ab(cc, i):
+        at = pl.multiple_of((cc * 4 + i) * KP, KP)
+        return local(7 + i, ab_hbm.at[pl.ds(at, KP)], ab_v.at[i])
 
     def ld_bt(i):
         k, cc, h = i // 4, i // 2 % 2, i % 2
@@ -80,26 +81,27 @@
 
     for cp in (ld_a, ld_g, ld_r, ld_ql):
         cp.start()
-    for i in range(4):
-        ld_ab(i).start()
-    for i in range(2):
-        ld_bt(i).start()
-
-    def start_corr(n, _):
-        for b in range(4):
-            ld_corr(n, b).start()
-        return 0
-
-    lax.fori_loop(0, 8, start_corr, 0)
+    def large_loads():
+        def corr(n, _):
+            for b in range(4):
+                ld_corr(n, b).start()
+            return 0
+
+        lax.fori_loop(0, 8, corr, 0)
+        for i in range(4):
+            ld_ab(c, i).start()
+        for i in range(2):
+            ld_bt(i).start()
 
     barrier = pltpu.get_barrier_semaphore()
-    for dev in [d1(1), d1(2), d1(3), d2(1), d2(2), d2(3), dz(1), dz(2), dz(3), sib]:
+    for dev in (d1(1), d1(2), d1(3), d2(1), d2(3), dz(1), dz(3), sib):
         pl.semaphore_signal(barrier, inc=1, device_id=dev, device_id_type=MESH)
-    pl.semaphore_wait(barrier, 10)
+    pl.semaphore_wait(barrier, 8)
 
     left1, right1, far1 = mod4(p1 + 3), mod4(p1 + 1), mod4(p1 + 2)
     left2, right2, far2 = mod4(p2 + 3), mod4(p2 + 1), mod4(p2 + 2)
     place = {"o": p1, "l": left1, "r": right1, "f": far1}
+    place2 = {"o": p2, "l": left2, "r": right2, "f": far2}
 
     class Gather:
         def __init__(self, nm, blk, half):
@@ -156,6 +158,14 @@
                 recv(self.nm + "2f" + b, self.blk(far2, place[b]))
             self.share(2)
 
+        def far_block(self, b):
+            ref = self.blk(far2, place[b])
+            recv(self.nm + "2f" + b, ref)
+            self._send("s2" + b, ref, sib)
+
+        def shared_block(self, b):
+            recv(self.nm + "s2" + b, self.blk(far1, place2[b], other))
+
         def shared(self, k):
             recv(f"{self.nm}s{k}", self.row(other, mod4(p1 + k)))
 
@@ -175,26 +185,29 @@
         return g
 
     g0, g1 = gather_g(0), gather_g(1)
-    gt = Gather("t", lambda row, at: arbuf.at[c, row, at],
+    gt = Gather("t", lambda row, at, cc=c: arbuf.at[cc, row, at],
                  lambda at, h: arbuf.at[c, p2, at, pl.ds(h * (TG // 2), TG // 2)])
     gt.row = lambda cc, row: arbuf.at[cc, row]
 
-    def act_rot():
+    def act_half(cc, more):
+        total = None
+        for i in range(4):
+            ld_ab(0, i).wait()
+            av = abuf[cc, :, :, :, i * KP:(i + 1) * KP].reshape(TG, KP)
+            part = jnp.dot(av, ab_v[i], preferred_element_type=F32)
+            total = part if i == 0 else total + part
+            if more:
+                ld_ab(other, i).start()
+        act_v[cc] = total
+
+    def act_rot_own():
+        act_half(c, True)
+
+    def act_rot_other():
         ga.all_shared()
-        for i in range(8):
-            cc = i // 4
-            ld_ab(i).wait()
-            av = abuf[cc, :, :, :, i % 4 * KP:(i % 4 + 1) * KP]
-            if cc == 1:
-                av = jnp.swapaxes(av, 0, 1)
-            part = jnp.dot(av.reshape(TG, KP), ab_v[i % 4], preferred_element_type=F32)
-            if i == 0:
-                act_v[...] = part
-            else:
-                act_v[...] += part
-            if i < 4:
-                ld_ab(i + 4).start()
-        arbuf[c, p2, p1] = act_v[...].astype(BF16)
+        act_half(other, False)
+        turned = jnp.swapaxes(act_v[1].reshape(4, 4, 16, DL), 0, 1).reshape(TG, DL)
+        arbuf[c, p2, p1] = (act_v[0] + turned).astype(BF16)
 
     def precond(second, n):
         at = 1 - pair if second else pair
@@ -203,19 +216,19 @@
             for b in range(4):
                 ld_corr(n, b).wait()
 
-        def one(b, _):
+        for b in range(4):
             corr = pbuf[n, b, pl.ds(pl.multiple_of((1 - pair) * QP, QP), FL)]
-            inv_v[...] = 1.0 / (corr.astype(F32) + 0.1)
-            right = rbuf[cc, at, row, b].reshape(2 * R, DL)
-            for q in range(2):
-                prod = jnp.dot(lbd[at, q * FL:(q + 1) * FL], right, preferred_element_type=F32)
-                pbuf[n, b, pl.ds(pl.multiple_of(at * QP + q * FL, FL), FL)] = (prod * inv_v[...]).astype(BF16)
-            return 0
-
-        lax.fori_loop(0, 4, one, 0)
+            inv_v[b] = 1.0 / (corr.astype(F32) + 0.1)
+        right = jnp.concatenate([rbuf[cc, at, row, b].reshape(2 * R, DL) for b in range(4)], axis=1)
+        for q in range(2):
+            prod = jnp.dot(lbd[at, q * FL:(q + 1) * FL], right, preferred_element_type=F32)
+            for b in range(4):
+                pbuf[n, b, pl.ds(pl.multiple_of(at * QP + q * FL, FL), FL)] = (
+                    prod[:, b * DL:(b + 1) * DL] * inv_v[b]).astype(BF16)
 
     def preconds(second, lo, hi):
-        lax.fori_loop(lo, hi, lambda n, _: (precond(second, n), 0)[1], 0)
+        for n in range(lo, hi):
+            precond(second, n)
 
     def grad_piece(i):
         k, cc, h = i // 4, i // 2 % 2, i % 2
@@ -232,18 +245,15 @@
             ld_bt(i + 2).start()
 
     def applied(groups):
-        def group(i, _):
-            cc, row = groups[0]
-            for at, (cc_at, row_at) in enumerate(groups):
-                cc, row = jnp.where(i == at, cc_at, cc), jnp.where(i == at, row_at, row)
-            rhs = jnp.concatenate([arbuf[cc, row, b] for b in range(4)], axis=1)
-            for m in range(7):
-                rows = slice(m * 256, (m + 1) * 256)
-                lhs = jnp.concatenate([pbuf[cc * 4 + row, b, rows] for b in range(4)], axis=1)
-                acc_v[rows] += lax.dot_general(lhs, rhs, NT, preferred_element_type=F32)
-            return 0
-
-        lax.fori_loop(0, len(groups), group, 0)
+        for cc, row in groups:
+            applied_blocks(cc, row, range(4))
+
+    def applied_blocks(cc, row, ats):
+        rhs = jnp.concatenate([arbuf[cc, row, at] for at in ats], axis=1)
+        for m in range(7):
+            rows = slice(m * 256, (m + 1) * 256)
+            lhs = jnp.concatenate([pbuf[cc * 4 + row, at, rows] for at in ats], axis=1)
+            acc_v[rows] += lax.dot_general(lhs, rhs, NT, preferred_element_type=F32)
 
     def share_pair(k):
         ref = rbuf.at[c, 1 - pair, :, :, k // 2]
@@ -280,12 +290,21 @@
         ld_r.wait()
         for k in (1, 3, 2):
             recv(f"r1{k}", rbuf.at[c, pair, p2, mod4(p1 - k)])
-        for k in (1, 3, 2):
-            send(f"r2{k}", rbuf.at[c, pair, p2], rbuf.at[c, pair, p2], d2(k))
+        for k, dev in (("+", d2(1)), ("-", d2(3))):
+            send("r2" + k, rbuf.at[c, pair, p2], rbuf.at[c, pair, p2], dev)
+
+    def right_half(row, h):
+        return rbuf.at[c, pair, row, pl.ds(2 * h, 2)]
+
+    def right_forward():
+        recv("r2+", rbuf.at[c, pair, left2])
+        send("r2f+", right_half(left2, 0), right_half(left2, 0), d2(1))
+        recv("r2-", rbuf.at[c, pair, right2])
+        send("r2f-", right_half(right2, 1), right_half(right2, 1), d2(3))
 
     def right_along_z():
-        for k in (1, 3, 2):
-            recv(f"r2{k}", rbuf.at[c, pair, mod4(p2 - k)])
+        recv("r2f+", right_half(far2, 0))
+        recv("r2f-", right_half(far2, 1))
         for k in (1, 3):
             ref = rbuf.at[c, pair, :, :, k // 2]
             send(f"rz{k}", ref, ref, dz(k))
@@ -295,119 +314,137 @@
     for k in (1, 3, 2):
         send(f"r1{k}", r_own, rbuf.at[c, pair, p2, p1], d1(k))
     send("sg", g_hbm.at[:, pl.ds(pl.multiple_of(other * KG, KG), KG)], g_in.at[c], sib)
-    left_factors()
     own_activations()
     ga.first()
     own_out_grads()
     g0.first()
     right_rows()
+    ga.first_forward("r")
     ga.second("o")
-    ga.first_forward("r")
+    large_loads()
+    ga.second("r")
     ga.first_forward("l")
     ga.second("l")
-    g0.first_forward("r")
     ga.first_far()
     ga.second("f")
+    left_factors()
+    right_forward()
+    g0.first_forward("l")
+    g0.first_forward("r")
+    ga.forward("l")
+    ga.forward("o")
+    g1.first()
+    ga.forward("r")
+    ga.near_row("r")
+    ga.forward("f")
+    g0.second("l")
+    g0.second("r")
     ga.share(0)
-    g0.first_forward("l")
-    ga.second("r")
     right_along_z()
     recv("rs0", rbuf.at[other, pair])
+    g0.second("o")
     preconds(False, 0, 2)
-    ga.forward("o")
-    ga.forward("l")
-    g1.first()
-    ga.forward("r")
-    ga.forward("f")
     ga.near_row("l")
-    g0.second("l")
+    ga.far_row()
     g0.first_far()
     g0.second("f")
-    g0.second("r")
     preconds(False, 2, 4)
-    share_pair(1)
-    g0.second("o")
-    share_pair(3)
     g1.first_forward("l")
     g1.second("l")
     g1.first_forward("r")
+    g1.second("r")
+    act_rot_own()
+    act_rot_other()
+    gt.first()
+    preconds(False, 4, 6)
+    share_pair(3)
+    g0.forward("f")
+    share_pair(1)
     g1.second("o")
-    g1.second("r")
-    ga.near_row("r")
-    ga.far_row()
+    g0.forward("r")
+    preconds(False, 6, 8)
+    g0.forward("o")
+    g1.first_far()
+    g0.forward("l")
+    g1.share(0)
+    g0.near_row("r")
+    gt.second("o")
+    gt.first_forward("r")
+    gt.first_forward("l")
     for k in (1, 3):
         recv(f"rs{k}", rbuf.at[other, 1 - pair, :, :, k // 2])
-    preconds(False, 4, 6)
-    g0.forward("l")
-    act_rot()
-    gt.second("o")
-    g0.forward("r")
-    gt.first()
-    preconds(True, 0, 4)
-    g0.forward("f")
-    preconds(False, 6, 8)
-    g0.forward("o")
-    g0.near_row("r")
+    preconds(True, 0, 2)
     g0.share(0)
-    gt.first_forward("r")
-    gt.first_forward("l")
+    gt.second("l")
+    preconds(True, 2, 4)
     g0.near_row("l")
-    g1.first_far()
-    g1.share(0)
+    preconds(True, 4, 6)
+    gt.second("r")
     g1.second("f")
-    preconds(True, 4, 6)
-    gt.second("l")
-    preconds(True, 6, 8)
     gt.first_far()
     gt.second("f")
-    gt.second("r")
+    gt.share(0)
     g1.forward("l")
+    preconds(True, 6, 8)
     g1.forward("o")
     g0.far_row()
-    gt.share(0)
-    applied([(c, p2)])
+    gt.shared(0)
+    applied([(other, p1)])
     g1.forward("r")
-    g1.near_row("r")
     g0.all_shared()
+    gt.forward("l")
     grad_piece(0)
     grad_piece(1)
-    gt.shared(0)
+    applied([(c, p2)])
+    gt.forward("r")
     g1.forward("f")
     g1.near_row("l")
-    gt.forward("o")
-    gt.forward("l")
-    applied([(other, p1)])
+    g1.near_row("r")
     grad_piece(2)
     grad_piece(3)
+    gt.forward("o")
     gt.forward("f")
     gt.near_row("l")
     applied([(c, left2)])
-    gt.forward("r")
     gt.near_row("r")
     applied([(c, right2)])
     g1.far_row()
     gt.shared(3)
     applied([(other, left1)])
+    gt.far_block("l")
     gt.shared(1)
-    applied([(other, right1)])
+    gt.far_block("o")
+    applied_blocks(c, far2, (p1, left1))
     g1.all_shared()
     grad_piece(4)
     grad_piece(5)
-    gt.far_row()
-    applied([(c, far2)])
+    gt.far_block("f")
+    gt.far_block("r")
+    applied([(other, right1)])
     grad_piece(6)
     grad_piece(7)
-    gt.shared(2)
-    applied([(other, far1)])
-
-    gr = gr_v[...]
-    sc = [jnp.sum(acc_v[q * FL:(q + 1) * FL] * gr, axis=0, keepdims=True) for q in range(Q)]
-    sc = jnp.concatenate(sc, axis=0)
+    gt.shared_block("o")
+    gt.shared_block("l")
+    gt.shared_block("f")
+    gt.shared_block("r")
+    applied_blocks(other, far1, (right2, far2))
+    applied_blocks(other, far1, (p2, left2))
+    applied_blocks(c, far2, (right1, far1))
+
+    sums = [jnp.zeros((8, TG), F32)] * Q
+    for i in range(FL // 8):
+        gr = gr_v[i * 8:(i + 1) * 8]
+        for q in range(Q):
+            sums[q] += acc_v[q * FL + i * 8:q * FL + (i + 1) * 8] * gr
+    sc = jnp.concatenate([jnp.sum(v, axis=0, keepdims=True) for v in sums], axis=0)
     place1 = x * 2 + c
     red1[place1] = jnp.concatenate([sc[:, :128], sc[:, 128:]], axis=0)
     for k in range(1, 8):
         to = lax.rem(place1 + k, 8)
         send(f"s1{k}", red1.at[place1], red1.at[place1], {"eig": y * 8 + to})
+    for cp in sent:
+        cp.wait_send()
+    sent.clear()
     for k in range(1, 8):
         recv(f"s1{k}", red1.at[lax.rem(place1 + 8 - k, 8)])
     red2[z, y] = jnp.sum(red1[...], axis=0)
@@ -416,6 +453,8 @@
             if kz or ky:
                 send(f"s2{kz}{ky}", red2.at[z, y], red2.at[z, y],
                      {"grp": mod4(z + kz), "eig": mod4(y + ky) * 8 + place1})
+    for cp in sent:
+        cp.wait_send()
     for kz in range(4):
         for ky in range(4):
             if kz or ky:
@@ -424,8 +463,6 @@
         total = jnp.sum(red2[g], axis=0)
         for half in range(2):
             out_ref[:, g * TG + half * 128:g * TG + (half + 1) * 128] = total[half * 4:half * 4 + 4]
-    for cp in sent:
-        cp.wait_send()
     assert len(tags) <= NSEM, len(tags)
 
 
@@ -448,8 +485,8 @@
             pltpu.VMEM((4, KP, DL), BF16),
             pltpu.VMEM((Q, R, FL), BF16),
             pltpu.VMEM((2, QP, 2 * R), BF16),
-            pltpu.VMEM((FL, DL), F32),
-            pltpu.VMEM((TG, DL), F32),
+            pltpu.VMEM((4, FL, DL), F32),
+            pltpu.VMEM((2, TG, DL), F32),
             pltpu.VMEM((FL, TG), F32),
             pltpu.VMEM((QI, TG), F32),
             pltpu.VMEM((8, 8, 128), F32),

time: 75.3 us -> 73.1 us (0.971)
  Pallas kernels: 73.8 us -> 71.6 us
    pallas_call x1, Pallas kernels: 73.8 us -> 71.6 us  [per_device(): pl.pallas_call(body, out_shape=jax.ShapeDtypeStruct((Q, T), F32), in_spec...]
where the time goes in v3:
time: 73.1 us; the launch traced here: 73 us
  Pallas kernels  71.6 us (98%)
  local copies, waits for them, and re-layouts  1.32 us (2%)
    pallas_call x1, Pallas kernels, per_device(): pl.pallas_call(body, out_shape=jax.ShapeDtypeStruct((Q, T), F32), in_spec...  71.6 us

profile of v3, /device:TPU:1, one launch (start us, length us, event | category | flops | bytes accessed | tf_op | source)
XLA Modules:
  0.0 73.0 jit_solution(6038401482466585458)
XLA Ops:
  0.0 71.6 %shard_map.73 = f32[4,1024]{1,0:T(4,128)} custom-call(bf16[8,8192]{1,0:T(8,128)(2,1)} %a_hbm.1, bf16[8,14336]{1,0:T(8,128)(2,1)} %g_hbm.1, bf16[448,14336]{1,0:T(8,128)(2,1)} %bitcast.2, bf16[8192,256]{1,0:T(8,128)(2,1)} %ab_hbm.1, bf16[448,8192]{1,0:T(8,128)(2,1)} %corr_hbm.1, bf16[4,32,448]{2,1,0:T(8,128)(2,1)} %ql_hbm.1, bf16[4,32,256]{2,1,0:T(8,128)(2,1)} %qr_hbm.1), custom_call_target="tpu_custom_call" | custom-call | tf_op jit(solution)/shard_map/pallas_call | solution.py:471
  71.7 1.3 %copy.9 = f32[1024,4]{0,1:T(4,128)} copy(f32[1024,4]{0,1:T(4,128)} %bitcast.3) | data formatting | bytes 32768

commit v4 on v3

--- a/solution.py
+++ b/solution.py
@@ -87,9 +87,9 @@
                 ld_corr(n, b).start()
             return 0
 
-        lax.fori_loop(0, 8, corr, 0)
         for i in range(4):
             ld_ab(c, i).start()
+        lax.fori_loop(0, 8, corr, 0)
         for i in range(2):
             ld_bt(i).start()
 
@@ -439,7 +439,7 @@
     sc = jnp.concatenate([jnp.sum(v, axis=0, keepdims=True) for v in sums], axis=0)
     place1 = x * 2 + c
     red1[place1] = jnp.concatenate([sc[:, :128], sc[:, 128:]], axis=0)
-    for k in range(1, 8):
+    for k in (4, 5, 3, 6, 2, 1, 7):
         to = lax.rem(place1 + k, 8)
         send(f"s1{k}", red1.at[place1], red1.at[place1], {"eig": y * 8 + to})
     for cp in sent:
@@ -448,8 +448,8 @@
     for k in range(1, 8):
         recv(f"s1{k}", red1.at[lax.rem(place1 + 8 - k, 8)])
     red2[z, y] = jnp.sum(red1[...], axis=0)
-    for kz in range(4):
-        for ky in range(4):
+    for kz in (2, 1, 3, 0):
+        for ky in (2, 1, 3, 0):
             if kz or ky:
                 send(f"s2{kz}{ky}", red2.at[z, y], red2.at[z, y],
                      {"grp": mod4(z + kz), "eig": mod4(y + ky) * 8 + place1})

time: 73.1 us -> 73.3 us (level)
  no operation moved by 1% of the time
where the time goes in v4:
time: 73.3 us; the launch traced here: 73.1 us
  Pallas kernels  71.8 us (98%)
  local copies, waits for them, and re-layouts  1.32 us (2%)
    pallas_call x1, Pallas kernels, per_device(): pl.pallas_call(body, out_shape=jax.ShapeDtypeStruct((Q, T), F32), in_spec...  71.8 us

profile of v4, /device:TPU:1, one launch (start us, length us, event | category | flops | bytes accessed | tf_op | source)
XLA Modules:
  0.0 73.1 jit_solution(16748546399101153175)
XLA Ops:
  0.0 71.8 %shard_map.73 = f32[4,1024]{1,0:T(4,128)} custom-call(bf16[8,8192]{1,0:T(8,128)(2,1)} %a_hbm.1, bf16[8,14336]{1,0:T(8,128)(2,1)} %g_hbm.1, bf16[448,14336]{1,0:T(8,128)(2,1)} %bitcast.2, bf16[8192,256]{1,0:T(8,128)(2,1)} %ab_hbm.1, bf16[448,8192]{1,0:T(8,128)(2,1)} %corr_hbm.1, bf16[4,32,448]{2,1,0:T(8,128)(2,1)} %ql_hbm.1, bf16[4,32,256]{2,1,0:T(8,128)(2,1)} %qr_hbm.1), custom_call_target="tpu_custom_call" | custom-call | tf_op jit(solution)/shard_map/pallas_call | solution.py:471
  71.8 1.3 %copy.9 = f32[1024,4]{0,1:T(4,128)} copy(f32[1024,4]{0,1:T(4,128)} %bitcast.3) | data formatting | bytes 32768
